TPU v7x, 32 devices: a whole 2x2x4 slice. The times are simulated.
32 devices in a mesh: ctx: 16 (over z, y, x), head: 2 (over core).
Axes of the slice: x: 2, y: 2, z: 4, core: 2. Of those that a mesh axis runs over, the one named last changes fastest.
Arguments:
- query: bfloat16 [4096, 8192], P(('ctx', 'head')), may hold values from -20 to 20
- key: bfloat16 [4096, 1024], P(('ctx', 'head')), may hold values from -6 to 6
- value: bfloat16 [4096, 1024], P(('ctx', 'head')), may hold values from -6 to 6
- doc_lengths: int32 [4], replicated, may hold values from 256 to 2048, as said below
- block_place: int32 [256], replicated, may hold values from 0 to 255, as said below
Outputs:
- attended: bfloat16 [4096, 8192], P('ctx', 'head')
Inputs may be any that keep to these rules, and one draw needn't show every extreme that they name: `doc_lengths`: 4 lengths that sum to 4096; the longest is exactly 2048 and the shortest exactly 256. `block_place`: A permutation of the blocks. The 8 blocks of one loading device (one index of ctx+head, ctx slowest) go to distinct context shards; context shard s holds packed blocks s * 16 to (s + 1) * 16 - 1.
All inputs are finite; a program needn't handle non-finite values.
Results may differ from a plain program's by a relative error of at most 0.0028.
Values may be sent and summed in bfloat16 or wider, within the bound.
No kernel may reach another device: no remote copies, remote signals or barrier semaphores. Data moves between devices by JAX's collectives and lax.ppermute only.
A program may use at most 192 MiB of HBM per device.

v0:
```python
import functools

import jax
import jax.numpy as jnp
import numpy as np
from jax import lax
from jax.experimental import pallas as pl
from jax.experimental.pallas import tpu as pltpu
from jax.sharding import Mesh
from jax.sharding import PartitionSpec as P

HD = 128
SPAN = 8
CHUNKS = (4, 4)
MASKED = -1e30
EXP2_SCALE = float(HD ** (-0.5) * np.log2(np.e))
VMEM_LIMIT = 60 * 1024 * 1024
ANY = pl.BlockSpec(memory_space=pl.ANY)


def whole(shape):
    return pl.BlockSpec(shape, lambda i, *_: (0,) * len(shape))


def call(kernel, scalars, arrays, in_specs, outs, out_specs, scratch, name, **more):
    return pl.pallas_call(
        kernel,
        out_shape=outs,
        grid_spec=pltpu.PrefetchScalarGridSpec(
            num_scalar_prefetch=len(scalars),
            grid=(1,),
            in_specs=in_specs,
            out_specs=out_specs,
            scratch_shapes=scratch,
        ),
        compiler_params=pltpu.CompilerParams(vmem_limit_bytes=VMEM_LIMIT),
        name=name,
        **more,
    )(*scalars, *arrays)


def moved(count):
    return pl.CostEstimate(flops=0, transcendentals=0, bytes_accessed=count)


def run_all(pairs, sems):
    copies = []
    for at, (source, target) in enumerate(pairs):
        copy = pltpu.make_async_copy(source, target, sems.at[at])
        copy.start()
        copies.append(copy)
    for copy in copies:
        copy.wait()


def split_kernel(near, query, key, value, first, later, sems):
    key_heads = first.shape[0]
    group = query.shape[1] // key_heads
    early = CHUNKS[0] * HD
    pairs = []
    for at in range(key_heads):
        head = at % 2 * near + at // 2
        start = head * group
        own = pl.ds(head * HD, HD)
        pairs.append((key.at[:, own], first.at[at, :, pl.ds(0, HD)]))
        pairs.append((value.at[:, own], first.at[at, :, pl.ds(HD, HD)]))
        pairs.append((query.at[:, pl.ds(start, early)], first.at[at, :, pl.ds(2 * HD, early)]))
        pairs.append((query.at[:, pl.ds(start + early, group - early)], later.at[at]))
    run_all(pairs, sems)


def split(query, key, value, near):
    rows, columns = query.shape
    key_heads = key.shape[1] // HD
    early = CHUNKS[0] * HD
    widths = (early + 2 * HD, columns // key_heads - early)
    return call(
        functools.partial(split_kernel, near),
        (),
        (query, key, value),
        [whole(query.shape), whole(key.shape), whole(value.shape)],
        [jax.ShapeDtypeStruct((key_heads, rows, width), query.dtype) for width in widths],
        [ANY] * 2,
        [pltpu.SemaphoreType.DMA((4 * key_heads,))],
        "split",
        cost_estimate=moved(4 * rows * (columns + 2 * key.shape[1])),
    )


def pack_kernel(offset, stride, source_ref, counts_ref, received, *refs):
    outs, (blocks, in_sem, sem) = refs[:-3], refs[-3:]
    run_all([(received.at[:, :, pl.ds(offset, blocks.shape[2])], blocks)], in_sem)
    for distance, out in enumerate(outs):

        def start(r, carry):
            source = source_ref[distance * stride + r]
            pltpu.make_async_copy(blocks.at[source], out.at[r], sem).start()
            return carry

        lax.fori_loop(0, counts_ref[distance], start, 0)
    pltpu.make_async_copy(blocks, blocks, sem).wait()


def pack(received, offset, width, sources, counts, capacity):
    total, block_rows, _ = received.shape
    far = counts.shape[0]
    stride = sources.shape[0] // far
    if block_rows % 16:
        packed = jnp.take(received[:, :, offset : offset + width], sources, axis=0)
        packed = packed.reshape(far, stride, block_rows, width)[:, :capacity]
        return [packed[at] for at in range(far)]
    return call(
        functools.partial(pack_kernel, offset, stride),
        (sources, counts),
        (received,),
        [ANY],
        [jax.ShapeDtypeStruct((capacity, block_rows, width), received.dtype)] * far,
        [ANY] * far,
        [
            pltpu.VMEM((total, block_rows, width), received.dtype),
            pltpu.SemaphoreType.DMA((1,)),
            pltpu.SemaphoreType.DMA(()),
        ],
        "pack",
        cost_estimate=moved(4 * total * block_rows * width),
    )


def window_kernel(pieces, rows_ref, counts_ref, *refs):
    arrived, (keys, turned, held, sem) = refs[:pieces], refs[pieces:]
    count, block_rows, _ = held.shape
    limit = arrived[0].shape[0]
    for at, piece in enumerate(arrived):

        def start(b, carry):
            row = rows_ref[at * limit + b]

            @pl.when(row >= 0)
            def _():
                pltpu.make_async_copy(piece.at[b], held.at[row], sem).start()

            return carry

        lax.fori_loop(0, counts_ref[at], start, 0)
    turned[HD:] = jnp.ones((turned.shape[0] - HD, turned.shape[1]), turned.dtype)

    def wait(b, carry):
        pltpu.make_async_copy(held.at[0], held.at[0], sem).wait()
        return carry

    lax.fori_loop(0, counts_ref[pieces], wait, 0)
    each = 256 // block_rows
    for part in range(count // each):
        at = pl.ds(part * 256, 256)
        blocks_at = pl.ds(part * each, each)
        keys[at] = held[blocks_at, :, :HD].reshape(256, HD)
        turned[:HD, at] = held[blocks_at, :, HD:].reshape(256, HD).T


def window_rows(block_place, plane, far, count):
    total = block_place.shape[0] // far
    first = (plane + 1) * total - count
    hops = np.array(list(range(far)) + list(range(-1, -far, -1)), dtype=np.int32)
    planes = plane - hops
    real = (planes >= 0) & (planes < far)
    places = jnp.take(block_place.reshape(far, total), jnp.clip(planes, 0, far - 1), axis=0) - first
    inside = (places >= 0) & (places < count)
    places = jnp.where(inside, places, -1)
    counts = jnp.where(real, total, 0).astype(jnp.int32)
    moving = jnp.sum((inside & real[:, None]).astype(jnp.int32))
    return places.reshape(-1), jnp.concatenate([counts, moving[None]])


def pick_window(pair, count, block_place, plane, places, counts):
    far = lax.axis_size("far")
    total, block_rows, width = pair.shape
    rows = count * block_rows
    if block_rows % 16:
        first = (plane + 1) * total - count
        wanted = jnp.maximum(first + jnp.arange(count, dtype=jnp.int32), 0)
        loaded = jnp.argmax(wanted[:, None] == block_place[None, :], axis=1)
        gathered = lax.all_gather(pair, "far", tiled=True)
        window = jnp.take(gathered, loaded, axis=0).reshape(rows, width)
        turned = jnp.concatenate([window[:, HD:].T, jnp.ones((16, rows), window.dtype)])
        return window[:, :HD], turned, [pair]
    up, down = [pair], [pair]
    for _ in range(far - 1):
        up.append(lax.ppermute(up[-1], "far", [(p, p + 1) for p in range(far - 1)]))
        down.append(lax.ppermute(down[-1], "far", [(p + 1, p) for p in range(far - 1)]))
    pieces = up + down[1:]
    shapes = [(rows, HD), (HD + 16, rows)]
    keys, turned = call(
        functools.partial(window_kernel, len(pieces)),
        (places, counts),
        pieces,
        [ANY] * len(pieces),
        [jax.ShapeDtypeStruct(shape, pair.dtype) for shape in shapes],
        [whole(shape) for shape in shapes],
        [pltpu.VMEM((count, block_rows, width), pair.dtype), pltpu.SemaphoreType.DMA(())],
        "window",
        cost_estimate=moved(4 * rows * width),
    )
    return keys, turned, [up[1], down[1]]


def attend_kernel(
    near, stride, docs, heads, place_ref, counts_ref, lengths_ref, plane_ref, *refs
):
    far = counts_ref.shape[0]
    arrived, keys, turned = refs[:far], refs[far], refs[far + 1]
    outs, (queries, out, maxes, sums, sem, out_sems) = refs[far + 2 : -6], refs[-6:]
    blocks, block_rows, width = queries.shape
    rows = blocks * block_rows // near
    tile = rows
    window_tiles = keys.shape[0] // tile
    per_shard = blocks // near
    for distance, piece in enumerate(arrived):

        def start(r, carry):
            place = place_ref[distance * stride + r]
            pltpu.make_async_copy(piece.at[r], queries.at[place], sem).start()
            return carry

        lax.fori_loop(0, counts_ref[distance], start, 0)
    plane_rows = near * rows
    window_start = (plane_ref[0] + 1) * plane_rows - keys.shape[0]
    pltpu.make_async_copy(queries, queries, sem).wait()

    def shard(j, carry):
        first_row = plane_ref[0] * plane_rows + j * rows
        query_rows = first_row + lax.broadcasted_iota(jnp.int32, (1, rows), 1)
        starts = jnp.zeros((1, rows), jnp.int32)
        first_start = jnp.int32(0)
        end = jnp.int32(0)
        for d in range(docs):
            length = lengths_ref[d]
            end = end + length
            starts = starts + jnp.where(query_rows >= end, length, 0)
            first_start = first_start + jnp.where(first_row >= end, length, 0)
        diagonal = window_tiles - near + j
        first_tile = (first_start - window_start) // tile
        for h in range(heads):
            maxes[h] = jnp.full((1, rows), MASKED, jnp.float32)
            sums[h] = jnp.zeros(sums.shape[1:], jnp.float32)

        def step(index, count, masked, last):
            span = count * tile
            at = pl.ds(pl.multiple_of(index * tile, tile), span)
            tile_keys = keys[at]
            tile_turned = turned[:, at]
            if masked:
                key_rows = (
                    window_start + index * tile + lax.broadcasted_iota(jnp.int32, (span, rows), 0)
                )
                visible = (key_rows >= starts) & (key_rows <= query_rows)
            if last:
                later = starts >= first_row

            def score(h):
                query = queries[pl.ds(j * per_shard, per_shard), :, h * HD : (h + 1) * HD]
                return lax.dot_general(
                    tile_keys,
                    query.reshape(rows, HD),
                    (((1,), (1,)), ((), ())),
                    preferred_element_type=jnp.float32,
                )

            ahead = score(0)
            for h in range(heads):
                scores = ahead
                if h + 1 < heads:
                    ahead = score(h + 1)
                if masked:
                    scores = jnp.where(visible, scores, MASKED)
                old = maxes[h]
                if last:
                    old = jnp.where(later, MASKED, old)
                new = jnp.maximum(old, jnp.max(scores, axis=0, keepdims=True))
                scaled = new * EXP2_SCALE
                weights = jnp.exp2(scores * EXP2_SCALE - scaled).astype(jnp.bfloat16)
                factor = jnp.exp2(old * EXP2_SCALE - scaled)
                product = jnp.dot(tile_turned, weights, preferred_element_type=jnp.float32)
                total = sums[h] * factor + product
                if last:
                    result = total[:HD] / total[HD : HD + 1]
                    out[j, :, h * HD : (h + 1) * HD] = result.T.astype(out.dtype)
                else:
                    maxes[h] = new
                    sums[h] = total

        @pl.when(first_tile < diagonal)
        def _():
            step(first_tile, 1, True, False)

        between = jnp.maximum(diagonal - first_tile - 1, 0)

        @pl.when(between % 2 == 1)
        def _():
            step(first_tile + 1, 1, False, False)

        def middle(index, carry):
            step(first_tile + 1 + between % 2 + 2 * index, 2, False, False)
            return carry

        lax.fori_loop(0, between // 2, middle, 0)
        step(diagonal, 1, True, True)
        return carry

    lax.fori_loop(0, near, shard, 0)
    run_all([(out.at[plane_ref[1] ^ at], target) for at, target in enumerate(outs)], out_sems)


def attend(arrived, keys, turned, places, slots, counts, doc_lengths, position, near, rows):
    block_rows, width = arrived[0].shape[1:]
    far = counts.shape[0]
    blocks = slots.shape[0]
    stride = places.shape[0] // far
    if block_rows % 16:
        joined = jnp.take(jnp.concatenate(arrived), slots, axis=0).reshape(-1, 16, width)
        arrived = [joined]
        block_rows = 16
        blocks = stride = joined.shape[0]
        places = jnp.arange(blocks, dtype=jnp.int32)
        counts = jnp.full((1,), blocks, jnp.int32)
    heads = width // HD
    shape = (rows, width)
    pairs = near * rows * keys.shape[0] * heads
    return call(
        functools.partial(attend_kernel, near, stride, doc_lengths.shape[0], heads),
        (places, counts, doc_lengths, position),
        (*arrived, keys, turned),
        [ANY] * len(arrived) + [whole(keys.shape), whole(turned.shape)],
        [jax.ShapeDtypeStruct(shape, keys.dtype)] * near,
        [ANY] * near,
        [
            pltpu.VMEM((blocks, block_rows, width), keys.dtype),
            pltpu.VMEM((near, rows, width), keys.dtype),
            pltpu.VMEM((heads, 1, rows), jnp.float32),
            pltpu.VMEM((heads, HD + 16, rows), jnp.float32),
            pltpu.SemaphoreType.DMA(()),
            pltpu.SemaphoreType.DMA((near,)),
        ],
        "attend",
        cost_estimate=pl.CostEstimate(
            flops=4 * pairs * HD, transcendentals=pairs, bytes_accessed=4 * near * rows * width
        ),
    )


def join_kernel(near, index_ref, *refs):
    parts, out, sems = refs[:-2], refs[-2], refs[-1]
    group = out.shape[1] // near
    offset = 0
    pairs = []
    for at, part in enumerate(parts):
        width = part.shape[1]
        column = (index_ref[0] ^ (at % near)) * group + offset
        pairs.append((part, out.at[:, pl.ds(pl.multiple_of(column, HD), width)]))
        if at % near == near - 1:
            offset += width
    run_all(pairs, sems)


def join(parts, index, near):
    rows = parts[0].shape[0]
    shape = (rows, sum(part.shape[1] for part in parts))
    return call(
        functools.partial(join_kernel, near),
        (index[None],),
        parts,
        [ANY] * len(parts),
        jax.ShapeDtypeStruct(shape, parts[0].dtype),
        whole(shape),
        [pltpu.SemaphoreType.DMA((len(parts),))],
        "join",
        cost_estimate=moved(4 * shape[0] * shape[1]),
    )


def body(query, key, value, doc_lengths, block_place):
    far = lax.axis_size("far")
    near = lax.axis_size("near")
    cores = lax.axis_size("head")
    loaded_rows = query.shape[0]
    rows = loaded_rows * cores
    block_rows = rows // (far * near)
    shard_blocks = rows // block_rows
    plane_blocks = near * shard_blocks
    plane = lax.axis_index("far").astype(jnp.int32)
    most = near * cores * min(near, loaded_rows // block_rows)

    def across(parts, axis, size):
        return [parts[0]] + [
            lax.ppermute(parts[at], axis, [(d, d ^ at) for d in range(size)])
            for at in range(1, size)
        ]

    index = lax.axis_index("near").astype(jnp.int32)

    def in_plane(x):
        x = lax.all_to_all(x, ("near", "head"), split_axis=0, concat_axis=0, tiled=True)
        return x.reshape(plane_blocks, block_rows, -1)

    first, later = split(query, key, value, near)
    received = in_plane(first)
    loaded = jnp.arange(block_place.shape[0], dtype=jnp.int32)
    origin = loaded // plane_blocks
    target = block_place // plane_blocks
    course = origin * far + target
    ahead = (course[:, None] == course[None, :]) & (loaded[None, :] < loaded[:, None])
    rank = jnp.sum(ahead.astype(jnp.int32), axis=1)

    def where_sum(found, values):
        return jnp.sum(jnp.where(found, values[None, :], 0), axis=1)

    distances = jnp.arange(far, dtype=jnp.int32)[:, None]
    leaving = jnp.where(origin == plane, target ^ plane, far)
    landing = jnp.where(target == plane, origin ^ plane, far)
    ones = jnp.ones_like(loaded)
    leaving_counts = where_sum(distances == leaving[None, :], ones)
    landing_counts = where_sum(distances == landing[None, :], ones)
    window_blocks = SPAN * shard_blocks + plane_blocks
    wanted = (plane + 1) * plane_blocks - window_blocks + jnp.arange(window_blocks, dtype=jnp.int32)
    found = jnp.maximum(wanted, 0)[:, None] == block_place[None, :]

    every = jnp.arange(far * most, dtype=jnp.int32)[:, None]
    leaving_slot = leaving * most + rank
    landing_slot = landing * most + rank
    sources = where_sum(every == leaving_slot[None, :], loaded % plane_blocks)
    places = where_sum(every == landing_slot[None, :], block_place % plane_blocks)

    window_places, window_counts = window_rows(block_place, plane, far, window_blocks)
    held = (leaving_counts, landing_counts, sources, places, window_places, window_counts)
    received, held, position = lax.optimization_barrier(
        (received, held, jnp.stack([plane, index]))
    )
    leaving_counts, landing_counts, sources, places, window_places, window_counts = held

    def with_slots(capacity, received, later):
        slots = where_sum(
            found[window_blocks - plane_blocks :], landing * capacity + rank
        )

        def attended(arrived):
            return attend(
                arrived,
                keys,
                turned,
                places,
                slots,
                landing_counts,
                doc_lengths,
                position,
                near,
                rows,
            )

        def sent(received, offset, chunk):
            width = CHUNKS[chunk] * HD
            return list(pack(received, offset, width, sources, leaving_counts, capacity))

        pair = received[:, :, : 2 * HD]
        pair, received = lax.optimization_barrier((pair, received))
        keys, turned, hops = pick_window(
            pair, window_blocks, block_place, plane, window_places, window_counts
        )
        arrived = [across(sent(received, 2 * HD, 0), "far", far)]
        hops, later = lax.optimization_barrier((hops, later))
        received = in_plane(later)
        offset = 0
        for chunk in range(1, len(CHUNKS)):
            arrived.append(across(sent(received, offset, chunk), "far", far))
            offset += CHUNKS[chunk] * HD
        parts = []
        for chunk in arrived:
            parts += across(list(attended(chunk)), "near", near)
        return join(parts, index, near)

    sizes = sorted({most * 5 // 8, most * 3 // 4, most})
    fullest = jnp.max(rank) + 1
    chosen = sum((fullest > size).astype(jnp.int32) for size in sizes[:-1])
    return lax.switch(chosen, [functools.partial(with_slots, size) for size in sizes], received, later)


def solution(mesh):
    near = 4
    shape = (mesh.shape["ctx"] // near, near, mesh.shape["head"])
    planes = Mesh(mesh.devices.reshape(shape), ("far", "near", "head"))
    placed = (
        P(("far", "near", "head"), None),
        P(("far", "near", "head"), None),
        P(("far", "near", "head"), None),
        P(),
        P(),
    )
    return jax.shard_map(
        body, mesh=planes, in_specs=placed, out_specs=P(("far", "near"), "head"), check_vma=False
    )
```

profile of v0, /device:TPU:14, one launch (start us, length us, event | category | flops | bytes accessed | tf_op | source)
XLA Modules:
  0.0 179.7 jit_solution(17443096399221027317)
XLA Ops:
  0.0 3.4 %split.1 = (bf16[8,128,768]{2,1,0:T(8,128)(2,1)}, bf16[8,128,512]{2,1,0:T(8,128)(2,1)}) custom-call(bf16[128,8192]{1,0:T(8,128)(2,1)} %query.1, bf16[128,1024]{1,0:T(8,128)(2,1)} %key.1, bf16[128,1024]{1,0:T(8,128)(2,1)} %value.1), custom_call_target="tpu_custom_call" | custom-call | bytes 5242880 | tf_op jit(solution)/shard_map/split/pallas_call | solution.py:26
  3.5 4.3 %all-to-all-start.3 = ((bf16[8,128,768]{2,1,0:T(8,128)(2,1)}), bf16[8,128,768]{2,1,0:T(8,128)(2,1)S(1)}, u32[]{:S(2)}, u32[]{:S(2)}) async-start(bf16[8,128,768]{2,1,0:T(8,128)(2,1)} %get-tuple-element.181), calls=%async_computation.3 | async-start | bytes 3145728 | tf_op jit(solution)/shard_map/all_to_all | solution.py:401
  11.8 14.8 %all-to-all-done.3 = bf16[8,128,768]{2,1,0:T(8,128)(2,1)S(1)} async-done(((bf16[8,128,768]{2,1,0:T(8,128)(2,1)}), bf16[8,128,768]{2,1,0:T(8,128)(2,1)S(1)}, u32[]{:S(2)}, u32[]{:S(2)}) %all-to-all-start.3) | async-done | bytes 1572896 | tf_op jit(solution)/shard_map/all_to_all | solution.py:401
  26.5 151.9 %conditional.1 = (bf16[256,4096]{1,0:T(8,128)(2,1)S(1)}) conditional(s32[]{:T(128)} %clamp.4, (s32[]{:T(128)}, bf16[64,16,768]{2,1,0:T(8,128)(2,1)S(1)}, s32[128]{0:T(128)S(1)}, s32[4]{0:T(128)S(1)}, s32[448]{0:T(512)S(1)}, /*index=5*/s32[8]{0:T(128)S(1)}, s32[128]{0:T(128)S(1)}, s32[4]{0:T(128)S(1)}, s32[4]{0:T(128)S(1)}, ...), branch_computations={%region_7.8_spmd, %region_8.9_spmd, %region_9.10_spmd} | conditional | flops 12884901888 | bytes 74450016 | solution.py:482
  26.6 3.5 %collective-permute-start.3 = (bf16[64,16,256]{2,1,0:T(8,128)(2,1)S(1)}, bf16[64,16,256]{2,1,0:T(8,128)(2,1)}, u32[]{:S(2)}, u32[]{:S(2)}) collective-permute-start(bf16[64,16,256]{2,1,0:T(8,128)(2,1)S(1)} %slice.6.refs_0_), channel_id=1, source_target_pairs={{0,8},{8,16},{16,24},{1,9},{9,17},{17,25},{2,10},{10,18},{18,26},{... | collective-permute-start | bytes 1572872 | tf_op jit(solution)/shard_map/cond/branch_0_fun/ppermute | solution.py:188
  30.1 3.1 %collective-permute-start.6 = (bf16[64,16,256]{2,1,0:T(8,128)(2,1)S(1)}, bf16[64,16,256]{2,1,0:T(8,128)(2,1)}, u32[]{:S(2)}, u32[]{:S(2)}) collective-permute-start(bf16[64,16,256]{2,1,0:T(8,128)(2,1)S(1)} %slice.6.refs_0_), channel_id=1, source_target_pairs={{8,0},{16,8},{24,16},{9,1},{17,9},{25,17},{10,2},{18,10},{26,18},{... | collective-permute-start | bytes 1572872 | tf_op jit(solution)/shard_map/cond/branch_0_fun/ppermute | solution.py:189
  33.2 9.0 %collective-permute-done.3.refs_1_ = bf16[64,16,256]{2,1,0:T(8,128)(2,1)} collective-permute-done((bf16[64,16,256]{2,1,0:T(8,128)(2,1)S(1)}, bf16[64,16,256]{2,1,0:T(8,128)(2,1)}, u32[]{:S(2)}, u32[]{:S(2)}) %collective-permute-start.3) | collective-permute-done | bytes 524320 | tf_op jit(solution)/shard_map/cond/branch_0_fun/ppermute | solution.py:188
  42.2 3.5 %collective-permute-start.4 = (bf16[64,16,256]{2,1,0:T(8,128)(2,1)}, bf16[64,16,256]{2,1,0:T(8,128)(2,1)}, u32[]{:S(2)}, u32[]{:S(2)}) collective-permute-start(bf16[64,16,256]{2,1,0:T(8,128)(2,1)} %collective-permute-done.3.refs_1_), channel_id=1, source_target_pairs={{0,8},{8,16},{16,24},{1,9},{9,17},{17,25},{2,10},{10,18},{18,26},{... | collective-permute-start | bytes 1572872 | tf_op jit(solution)/shard_map/cond/branch_0_fun/ppermute | solution.py:188
  45.7 3.2 %collective-permute-start.7 = (bf16[64,16,256]{2,1,0:T(8,128)(2,1)}, bf16[64,16,256]{2,1,0:T(8,128)(2,1)}, u32[]{:S(2)}, u32[]{:S(2)}) collective-permute-start(bf16[64,16,256]{2,1,0:T(8,128)(2,1)} %collective-permute-done.6.refs_4_), channel_id=1, source_target_pairs={{8,0},{16,8},{24,16},{9,1},{17,9},{25,17},{10,2},{18,10},{26,18},{... | collective-permute-start | bytes 1572872 | tf_op jit(solution)/shard_map/cond/branch_0_fun/ppermute | solution.py:189
  48.8 4.4 %all-to-all-start = ((bf16[8,128,512]{2,1,0:T(8,128)(2,1)}), bf16[8,128,512]{2,1,0:T(8,128)(2,1)S(1)}, u32[]{:S(2)}, u32[]{:S(2)}) async-start(bf16[8,128,512]{2,1,0:T(8,128)(2,1)} %get-tuple-element.98), calls=%async_computation | async-start | bytes 2097152 | tf_op jit(solution)/shard_map/cond/branch_0_fun/all_to_all | solution.py:401
  53.3 3.8 %collective-permute-done.4.refs_2_ = bf16[64,16,256]{2,1,0:T(8,128)(2,1)} collective-permute-done((bf16[64,16,256]{2,1,0:T(8,128)(2,1)}, bf16[64,16,256]{2,1,0:T(8,128)(2,1)}, u32[]{:S(2)}, u32[]{:S(2)}) %collective-permute-start.4) | collective-permute-done | bytes 524320 | tf_op jit(solution)/shard_map/cond/branch_0_fun/ppermute | solution.py:188
  57.1 3.5 %collective-permute-start.5 = (bf16[64,16,256]{2,1,0:T(8,128)(2,1)}, bf16[64,16,256]{2,1,0:T(8,128)(2,1)}, u32[]{:S(2)}, u32[]{:S(2)}) collective-permute-start(bf16[64,16,256]{2,1,0:T(8,128)(2,1)} %collective-permute-done.4.refs_2_), channel_id=1, source_target_pairs={{0,8},{8,16},{16,24},{1,9},{9,17},{17,25},{2,10},{10,18},{18,26},{... | collective-permute-start | bytes 1572872 | tf_op jit(solution)/shard_map/cond/branch_0_fun/ppermute | solution.py:188
  60.6 3.2 %collective-permute-start.8 = (bf16[64,16,256]{2,1,0:T(8,128)(2,1)}, bf16[64,16,256]{2,1,0:T(8,128)(2,1)}, u32[]{:S(2)}, u32[]{:S(2)}) collective-permute-start(bf16[64,16,256]{2,1,0:T(8,128)(2,1)} %collective-permute-done.7.refs_5_), channel_id=1, source_target_pairs={{8,0},{16,8},{24,16},{9,1},{17,9},{25,17},{10,2},{18,10},{26,18},{... | collective-permute-start | bytes 1572872 | tf_op jit(solution)/shard_map/cond/branch_0_fun/ppermute | solution.py:189
  65.6 2.6 %collective-permute-start.1 = (bf16[20,16,512]{2,1,0:T(8,128)(2,1)}, bf16[20,16,512]{2,1,0:T(8,128)(2,1)S(1)}, u32[]{:S(2)}, u32[]{:S(2)}) collective-permute-start(bf16[20,16,512]{2,1,0:T(8,128)(2,1)} %get-tuple-element.86), channel_id=1, source_target_pairs={{0,16},{8,24},{16,0},{24,8},{1,17},{9,25},{17,1},{25,9},{2,18},{10... | collective-permute-start | bytes 983048 | tf_op jit(solution)/shard_map/cond/branch_0_fun/ppermute | solution.py:394
  70.0 2.8 %pack.7 = (bf16[20,16,512]{2,1,0:T(8,128)(2,1)}, bf16[20,16,512]{2,1,0:T(8,128)(2,1)}, bf16[20,16,512]{2,1,0:T(8,128)(2,1)}, bf16[20,16,512]{2,1,0:T(8,128)(2,1)}) custom-call(s32[128]{0:T(128)S(1)} %get-tuple-element.80.source_ref, s32[4]{0:T(128)S(1)} %get-tuple-element.81.counts_ref, bf16[64,16,512]{2,1,0:T(8,128)(2,1)} %bitcast.13), custom_call_target="tpu_custom_call" | custom-call | bytes 2097152 | tf_op jit(solution)/shard_map/cond/branch_0_fun/pack/pallas_call | solution.py:26
  74.2 7.1 %collective-permute-done.8.refs_6_ = bf16[64,16,256]{2,1,0:T(8,128)(2,1)} collective-permute-done((bf16[64,16,256]{2,1,0:T(8,128)(2,1)}, bf16[64,16,256]{2,1,0:T(8,128)(2,1)}, u32[]{:S(2)}, u32[]{:S(2)}) %collective-permute-start.8) | collective-permute-done | bytes 524320 | tf_op jit(solution)/shard_map/cond/branch_0_fun/ppermute | solution.py:189
  81.7 4.5 %window.3 = (bf16[3072,128]{1,0:T(8,128)(2,1)}, bf16[144,3072]{1,0:T(8,128)(2,1)}) custom-call(s32[448]{0:T(512)S(1)} %get-tuple-element.88.rows_ref, s32[8]{0:T(128)S(1)} %get-tuple-element.89.counts_ref, bf16[64,16,256]{2,1,0:T(8,128)(2,1)} %copy-done.3, bf16[64,16,256]{2,1,0:T(8,128)(2,1)} %collective-permute-done.3.refs_1_, ...), custom_call_target="tpu_custom_call" | custom-call | bytes 3145728 | tf_op jit(solution)/shard_map/cond/branch_0_fun/window/pallas_call | solution.py:26
  86.2 8.3 %collective-permute-done.refs_1_ = bf16[20,16,512]{2,1,0:T(8,128)(2,1)S(1)} collective-permute-done((bf16[20,16,512]{2,1,0:T(8,128)(2,1)}, bf16[20,16,512]{2,1,0:T(8,128)(2,1)S(1)}, u32[]{:S(2)}, u32[]{:S(2)}) %collective-permute-start) | collective-permute-done | bytes 327712 | tf_op jit(solution)/shard_map/cond/branch_0_fun/ppermute | solution.py:394
  95.0 24.7 %collective-permute-done.2.refs_3_ = bf16[20,16,512]{2,1,0:T(8,128)(2,1)S(1)} collective-permute-done((bf16[20,16,512]{2,1,0:T(8,128)(2,1)}, bf16[20,16,512]{2,1,0:T(8,128)(2,1)S(1)}, u32[]{:S(2)}, u32[]{:S(2)}) %collective-permute-start.2) | collective-permute-done | bytes 327712 | tf_op jit(solution)/shard_map/cond/branch_0_fun/ppermute | solution.py:394
  120.4 20.0 %attend.6 = (bf16[256,512]{1,0:T(8,128)(2,1)}, bf16[256,512]{1,0:T(8,128)(2,1)}, bf16[256,512]{1,0:T(8,128)(2,1)}, bf16[256,512]{1,0:T(8,128)(2,1)}) custom-call(s32[128]{0:T(128)S(1)} %get-tuple-element.76.place_ref, s32[4]{0:T(128)S(1)} %get-tuple-element.77.counts_ref, s32[4]{0:T(128)S(1)} %get-tuple-element.78.lengths_ref, ...), custom_call_target="tpu_custom_call" | custom-call | flops 6442450944 | bytes 2097152 | tf_op jit(solution)/shard_map/cond/branch_0_fun/attend/pallas_call | solution.py:26
  140.5 2.2 %collective-permute-start.10 = (bf16[256,512]{1,0:T(8,128)(2,1)}, bf16[256,512]{1,0:T(8,128)(2,1)S(1)}, u32[]{:S(2)}, u32[]{:S(2)}) collective-permute-start(bf16[256,512]{1,0:T(8,128)(2,1)} %get-tuple-element.95), channel_id=1, source_target_pairs={{0,4},{2,6},{4,0},{6,2},{1,5},{3,7},{5,1},{7,3},{8,12},{10,14},{12... | collective-permute-start | bytes 786440 | tf_op jit(solution)/shard_map/cond/branch_0_fun/ppermute | solution.py:394
  145.0 20.0 %attend.7 = (bf16[256,512]{1,0:T(8,128)(2,1)}, bf16[256,512]{1,0:T(8,128)(2,1)}, bf16[256,512]{1,0:T(8,128)(2,1)}, bf16[256,512]{1,0:T(8,128)(2,1)}) custom-call(s32[128]{0:T(128)S(1)} %get-tuple-element.76.place_ref, s32[4]{0:T(128)S(1)} %get-tuple-element.77.counts_ref, s32[4]{0:T(128)S(1)} %get-tuple-element.78.lengths_ref, ...), custom_call_target="tpu_custom_call" | custom-call | flops 6442450944 | bytes 2097152 | tf_op jit(solution)/shard_map/cond/branch_0_fun/attend/pallas_call | solution.py:26
  168.6 3.1 %collective-permute-done.15.refs_5_ = bf16[256,512]{1,0:T(8,128)(2,1)S(1)} collective-permute-done((bf16[256,512]{1,0:T(8,128)(2,1)}, bf16[256,512]{1,0:T(8,128)(2,1)S(1)}, u32[]{:S(2)}, u32[]{:S(2)}) %collective-permute-start.15) | collective-permute-done | bytes 262176 | tf_op jit(solution)/shard_map/cond/branch_0_fun/ppermute | solution.py:394
  171.7 2.5 %collective-permute-done.16.refs_6_ = bf16[256,512]{1,0:T(8,128)(2,1)S(1)} collective-permute-done((bf16[256,512]{1,0:T(8,128)(2,1)}, bf16[256,512]{1,0:T(8,128)(2,1)S(1)}, u32[]{:S(2)}, u32[]{:S(2)}) %collective-permute-start.16) | collective-permute-done | bytes 262176 | tf_op jit(solution)/shard_map/cond/branch_0_fun/ppermute | solution.py:394
  (79 shorter events, 21.2 us)
Async XLA Ops:
  3.5 23.1 %copy-start.46 = (s32[4]{0:T(128)S(1)}, s32[4]{0:T(128)}, u32[]{:S(2)}) copy-start(s32[4]{0:T(128)} %param.12) | copy-start | bytes 52
  3.5 23.1 %all-to-all-start.3 = ((bf16[8,128,768]{2,1,0:T(8,128)(2,1)}), bf16[8,128,768]{2,1,0:T(8,128)(2,1)S(1)}, u32[]{:S(2)}, u32[]{:S(2)}) async-start(bf16[8,128,768]{2,1,0:T(8,128)(2,1)} %get-tuple-element.181), calls=%async_computation.3 | async-start | bytes 3145728 | tf_op jit(solution)/shard_map/all_to_all | solution.py:401
  26.6 46.3 %copy-start.3 = (bf16[64,16,256]{2,1,0:T(8,128)(2,1)}, bf16[64,16,256]{2,1,0:T(8,128)(2,1)S(1)}, u32[]{:S(2)}) copy-start(bf16[64,16,256]{2,1,0:T(8,128)(2,1)S(1)} %slice.6.refs_0_) | copy-start | bytes 1572868 | tf_op jit(solution)/shard_map/cond
  26.6 15.6 %collective-permute-start.3 = (bf16[64,16,256]{2,1,0:T(8,128)(2,1)S(1)}, bf16[64,16,256]{2,1,0:T(8,128)(2,1)}, u32[]{:S(2)}, u32[]{:S(2)}) collective-permute-start(bf16[64,16,256]{2,1,0:T(8,128)(2,1)S(1)} %slice.6.refs_0_), channel_id=1, source_target_pairs={{0,8},{8,16},{16,24},{1,9},{9,17},{17,25},{2,10},{10,18},{18,26},{... | collective-permute-start | bytes 1572872 | tf_op jit(solution)/shard_map/cond/branch_0_fun/ppermute | solution.py:188
  30.1 15.6 %collective-permute-start.6 = (bf16[64,16,256]{2,1,0:T(8,128)(2,1)S(1)}, bf16[64,16,256]{2,1,0:T(8,128)(2,1)}, u32[]{:S(2)}, u32[]{:S(2)}) collective-permute-start(bf16[64,16,256]{2,1,0:T(8,128)(2,1)S(1)} %slice.6.refs_0_), channel_id=1, source_target_pairs={{8,0},{16,8},{24,16},{9,1},{17,9},{25,17},{10,2},{18,10},{26,18},{... | collective-permute-start | bytes 1572872 | tf_op jit(solution)/shard_map/cond/branch_0_fun/ppermute | solution.py:189
  42.2 14.9 %collective-permute-start.4 = (bf16[64,16,256]{2,1,0:T(8,128)(2,1)}, bf16[64,16,256]{2,1,0:T(8,128)(2,1)}, u32[]{:S(2)}, u32[]{:S(2)}) collective-permute-start(bf16[64,16,256]{2,1,0:T(8,128)(2,1)} %collective-permute-done.3.refs_1_), channel_id=1, source_target_pairs={{0,8},{8,16},{16,24},{1,9},{9,17},{17,25},{2,10},{10,18},{18,26},{... | collective-permute-start | bytes 1572872 | tf_op jit(solution)/shard_map/cond/branch_0_fun/ppermute | solution.py:188
  45.7 14.9 %collective-permute-start.7 = (bf16[64,16,256]{2,1,0:T(8,128)(2,1)}, bf16[64,16,256]{2,1,0:T(8,128)(2,1)}, u32[]{:S(2)}, u32[]{:S(2)}) collective-permute-start(bf16[64,16,256]{2,1,0:T(8,128)(2,1)} %collective-permute-done.6.refs_4_), channel_id=1, source_target_pairs={{8,0},{16,8},{24,16},{9,1},{17,9},{25,17},{10,2},{18,10},{26,18},{... | collective-permute-start | bytes 1572872 | tf_op jit(solution)/shard_map/cond/branch_0_fun/ppermute | solution.py:189
  48.8 20.2 %all-to-all-start = ((bf16[8,128,512]{2,1,0:T(8,128)(2,1)}), bf16[8,128,512]{2,1,0:T(8,128)(2,1)S(1)}, u32[]{:S(2)}, u32[]{:S(2)}) async-start(bf16[8,128,512]{2,1,0:T(8,128)(2,1)} %get-tuple-element.98), calls=%async_computation | async-start | bytes 2097152 | tf_op jit(solution)/shard_map/cond/branch_0_fun/all_to_all | solution.py:401
  57.1 17.1 %collective-permute-start.5 = (bf16[64,16,256]{2,1,0:T(8,128)(2,1)}, bf16[64,16,256]{2,1,0:T(8,128)(2,1)}, u32[]{:S(2)}, u32[]{:S(2)}) collective-permute-start(bf16[64,16,256]{2,1,0:T(8,128)(2,1)} %collective-permute-done.4.refs_2_), channel_id=1, source_target_pairs={{0,8},{8,16},{16,24},{1,9},{9,17},{17,25},{2,10},{10,18},{18,26},{... | collective-permute-start | bytes 1572872 | tf_op jit(solution)/shard_map/cond/branch_0_fun/ppermute | solution.py:188
  60.6 20.6 %collective-permute-start.8 = (bf16[64,16,256]{2,1,0:T(8,128)(2,1)}, bf16[64,16,256]{2,1,0:T(8,128)(2,1)}, u32[]{:S(2)}, u32[]{:S(2)}) collective-permute-start(bf16[64,16,256]{2,1,0:T(8,128)(2,1)} %collective-permute-done.7.refs_5_), channel_id=1, source_target_pairs={{8,0},{16,8},{24,16},{9,1},{17,9},{25,17},{10,2},{18,10},{26,18},{... | collective-permute-start | bytes 1572872 | tf_op jit(solution)/shard_map/cond/branch_0_fun/ppermute | solution.py:189
  65.5 29.1 %collective-permute-start = (bf16[20,16,512]{2,1,0:T(8,128)(2,1)}, bf16[20,16,512]{2,1,0:T(8,128)(2,1)S(1)}, u32[]{:S(2)}, u32[]{:S(2)}) collective-permute-start(bf16[20,16,512]{2,1,0:T(8,128)(2,1)} %get-tuple-element.85), channel_id=1, source_target_pairs={{0,8},{8,0},{16,24},{24,16},{1,9},{9,1},{17,25},{25,17},{2,10},{10... | collective-permute-start | bytes 983048 | tf_op jit(solution)/shard_map/cond/branch_0_fun/ppermute | solution.py:394
  65.6 29.4 %collective-permute-start.1 = (bf16[20,16,512]{2,1,0:T(8,128)(2,1)}, bf16[20,16,512]{2,1,0:T(8,128)(2,1)S(1)}, u32[]{:S(2)}, u32[]{:S(2)}) collective-permute-start(bf16[20,16,512]{2,1,0:T(8,128)(2,1)} %get-tuple-element.86), channel_id=1, source_target_pairs={{0,16},{8,24},{16,0},{24,8},{1,17},{9,25},{17,1},{25,9},{2,18},{10... | collective-permute-start | bytes 983048 | tf_op jit(solution)/shard_map/cond/branch_0_fun/ppermute | solution.py:394
  68.2 51.5 %collective-permute-start.2 = (bf16[20,16,512]{2,1,0:T(8,128)(2,1)}, bf16[20,16,512]{2,1,0:T(8,128)(2,1)S(1)}, u32[]{:S(2)}, u32[]{:S(2)}) collective-permute-start(bf16[20,16,512]{2,1,0:T(8,128)(2,1)} %get-tuple-element.87), channel_id=1, source_target_pairs={{0,24},{8,16},{16,8},{24,0},{1,25},{9,17},{17,9},{25,1},{2,26},{10... | collective-permute-start | bytes 983048 | tf_op jit(solution)/shard_map/cond/branch_0_fun/ppermute | solution.py:394
  74.2 68.5 %collective-permute-start.12 = (bf16[20,16,512]{2,1,0:T(8,128)(2,1)}, bf16[20,16,512]{2,1,0:T(8,128)(2,1)S(1)}, u32[]{:S(2)}, u32[]{:S(2)}) collective-permute-start(bf16[20,16,512]{2,1,0:T(8,128)(2,1)} %get-tuple-element.100), channel_id=1, source_target_pairs={{0,8},{8,0},{16,24},{24,16},{1,9},{9,1},{17,25},{25,17},{2,10},{10... | collective-permute-start | bytes 983048 | tf_op jit(solution)/shard_map/cond/branch_0_fun/ppermute | solution.py:394
  81.2 63.0 %collective-permute-start.13 = (bf16[20,16,512]{2,1,0:T(8,128)(2,1)}, bf16[20,16,512]{2,1,0:T(8,128)(2,1)S(1)}, u32[]{:S(2)}, u32[]{:S(2)}) collective-permute-start(bf16[20,16,512]{2,1,0:T(8,128)(2,1)} %get-tuple-element.101), channel_id=1, source_target_pairs={{0,16},{8,24},{16,0},{24,8},{1,17},{9,25},{17,1},{25,9},{2,18},{10... | collective-permute-start | bytes 983048 | tf_op jit(solution)/shard_map/cond/branch_0_fun/ppermute | solution.py:394
  94.6 25.1 %copy-start.42 = (bf16[20,16,512]{2,1,0:T(8,128)(2,1)}, bf16[20,16,512]{2,1,0:T(8,128)(2,1)S(1)}, u32[]{:S(2)}) copy-start(bf16[20,16,512]{2,1,0:T(8,128)(2,1)S(1)} %collective-permute-done.refs_1_) | copy-start | bytes 983044 | tf_op jit(solution)/shard_map/cond
  94.6 49.6 %collective-permute-start.14 = (bf16[20,16,512]{2,1,0:T(8,128)(2,1)S(1)}, bf16[20,16,512]{2,1,0:T(8,128)(2,1)S(1)}, u32[]{:S(2)}, u32[]{:S(2)}) collective-permute-start(bf16[20,16,512]{2,1,0:T(8,128)(2,1)S(1)} %copy-done.40), channel_id=1, source_target_pairs={{0,24},{8,16},{16,8},{24,0},{1,25},{9,17},{17,9},{25,1},{2,26},{10... | collective-permute-start | bytes 983048 | tf_op jit(solution)/shard_map/cond/branch_0_fun/ppermute | solution.py:394
  95.0 24.7 %copy-start.43 = (bf16[20,16,512]{2,1,0:T(8,128)(2,1)}, bf16[20,16,512]{2,1,0:T(8,128)(2,1)S(1)}, u32[]{:S(2)}) copy-start(bf16[20,16,512]{2,1,0:T(8,128)(2,1)S(1)} %collective-permute-done.1.refs_2_) | copy-start | bytes 983044 | tf_op jit(solution)/shard_map/cond
  140.5 26.7 %collective-permute-start.10 = (bf16[256,512]{1,0:T(8,128)(2,1)}, bf16[256,512]{1,0:T(8,128)(2,1)S(1)}, u32[]{:S(2)}, u32[]{:S(2)}) collective-permute-start(bf16[256,512]{1,0:T(8,128)(2,1)} %get-tuple-element.95), channel_id=1, source_target_pairs={{0,4},{2,6},{4,0},{6,2},{1,5},{3,7},{5,1},{7,3},{8,12},{10,14},{12... | collective-permute-start | bytes 786440 | tf_op jit(solution)/shard_map/cond/branch_0_fun/ppermute | solution.py:394
  142.6 26.0 %collective-permute-start.11 = (bf16[256,512]{1,0:T(8,128)(2,1)}, bf16[256,512]{1,0:T(8,128)(2,1)S(1)}, u32[]{:S(2)}, u32[]{:S(2)}) collective-permute-start(bf16[256,512]{1,0:T(8,128)(2,1)} %get-tuple-element.96), channel_id=1, source_target_pairs={{0,6},{2,4},{4,2},{6,0},{1,7},{3,5},{5,3},{7,1},{8,14},{10,12},{12... | collective-permute-start | bytes 786440 | tf_op jit(solution)/shard_map/cond/branch_0_fun/ppermute | solution.py:394
  142.6 25.9 %collective-permute-start.9 = (bf16[256,512]{1,0:T(8,128)(2,1)}, bf16[256,512]{1,0:T(8,128)(2,1)S(1)}, u32[]{:S(2)}, u32[]{:S(2)}) collective-permute-start(bf16[256,512]{1,0:T(8,128)(2,1)} %get-tuple-element.94), channel_id=1, source_target_pairs={{0,2},{2,0},{4,6},{6,4},{1,3},{3,1},{5,7},{7,5},{8,10},{10,8},{12,... | collective-permute-start | bytes 786440 | tf_op jit(solution)/shard_map/cond/branch_0_fun/ppermute | solution.py:394
  165.0 6.6 %collective-permute-start.15 = (bf16[256,512]{1,0:T(8,128)(2,1)}, bf16[256,512]{1,0:T(8,128)(2,1)S(1)}, u32[]{:S(2)}, u32[]{:S(2)}) collective-permute-start(bf16[256,512]{1,0:T(8,128)(2,1)} %get-tuple-element.104), channel_id=1, source_target_pairs={{0,2},{2,0},{4,6},{6,4},{1,3},{3,1},{5,7},{7,5},{8,10},{10,8},{12,... | collective-permute-start | bytes 786440 | tf_op jit(solution)/shard_map/cond/branch_0_fun/ppermute | solution.py:394
  165.6 8.5 %collective-permute-start.16 = (bf16[256,512]{1,0:T(8,128)(2,1)}, bf16[256,512]{1,0:T(8,128)(2,1)S(1)}, u32[]{:S(2)}, u32[]{:S(2)}) collective-permute-start(bf16[256,512]{1,0:T(8,128)(2,1)} %get-tuple-element.105), channel_id=1, source_target_pairs={{0,4},{2,6},{4,0},{6,2},{1,5},{3,7},{5,1},{7,3},{8,12},{10,14},{12... | collective-permute-start | bytes 786440 | tf_op jit(solution)/shard_map/cond/branch_0_fun/ppermute | solution.py:394
  167.1 8.7 %collective-permute-start.17 = (bf16[256,512]{1,0:T(8,128)(2,1)}, bf16[256,512]{1,0:T(8,128)(2,1)S(1)}, u32[]{:S(2)}, u32[]{:S(2)}) collective-permute-start(bf16[256,512]{1,0:T(8,128)(2,1)} %get-tuple-element.106), channel_id=1, source_target_pairs={{0,6},{2,4},{4,2},{6,0},{1,7},{3,5},{5,3},{7,1},{8,14},{10,12},{12... | collective-permute-start | bytes 786440 | tf_op jit(solution)/shard_map/cond/branch_0_fun/ppermute | solution.py:394
  (15 other events, 66.6 us)
where the time goes:
time: 183 us; the launch traced here: 180 us
  waiting for transfers between devices  76.3 us (42%)
  Pallas kernels  54 us (30%)
  starting transfers between devices  40.4 us (22%)
  local copies, waits for them, and re-layouts  5.3 us (3%)
  other arithmetic  2.61 us (1%)
    pallas_call x7, Pallas kernels, call(): pl.pallas_call(kernel, out_shape=outs, grid_spec=pltpu.PrefetchScalarGrid...  54 us
    ppermute x12, waiting for transfers between devices, across(): lax.ppermute(parts[at], axis, [(d, d ^ at) for d in range(size)])  40.3 us
    all_to_all x2, waiting for transfers between devices, in_plane(): lax.all_to_all(x, ('near', 'head'), split_axis=0, concat_axis=0, tiled=True)  14.8 us
    ppermute x3, waiting for transfers between devices, pick_window(): up.append(lax.ppermute(up[-1], 'far', [(p, p + 1) for p in range(far - 1)]))  14.1 us
    ppermute x12, starting transfers between devices, across(): lax.ppermute(parts[at], axis, [(d, d ^ at) for d in range(size)])  11.8 us
    ppermute x3, starting transfers between devices, pick_window(): up.append(lax.ppermute(up[-1], 'far', [(p, p + 1) for p in range(far - 1)]))  10.4 us
    ppermute x3, starting transfers between devices, pick_window(): lax.ppermute(down[-1], 'far', [(p + 1, p) for p in range(far - 1)])  9.46 us
    all_to_all x2, starting transfers between devices, in_plane(): lax.all_to_all(x, ('near', 'head'), split_axis=0, concat_axis=0, tiled=True)  8.76 us
  transfers between devices with their start and end apart: 20, of which 10 were waited for; matrix products, arithmetic and copies ran while one was open for 2% of the time, Pallas kernels for 27%

commit v1 on v0

--- a/solution.py
+++ b/solution.py
@@ -171,7 +171,7 @@
     return places.reshape(-1), jnp.concatenate([counts, moving[None]])
 
 
-def pick_window(pair, count, block_place, plane, places, counts):
+def pick_window(pair, count, block_place, plane, places, counts, early):
     far = lax.axis_size("far")
     total, block_rows, width = pair.shape
     rows = count * block_rows
@@ -182,9 +182,11 @@
         gathered = lax.all_gather(pair, "far", tiled=True)
         window = jnp.take(gathered, loaded, axis=0).reshape(rows, width)
         turned = jnp.concatenate([window[:, HD:].T, jnp.ones((16, rows), window.dtype)])
-        return window[:, :HD], turned, [pair]
+        return window[:, :HD], turned, [pair], early
     up, down = [pair], [pair]
-    for _ in range(far - 1):
+    for hop in range(far - 1):
+        if hop == far - 2:
+            early, up[-1], down[-1] = lax.optimization_barrier((early, up[-1], down[-1]))
         up.append(lax.ppermute(up[-1], "far", [(p, p + 1) for p in range(far - 1)]))
         down.append(lax.ppermute(down[-1], "far", [(p + 1, p) for p in range(far - 1)]))
     pieces = up + down[1:]
@@ -200,7 +202,7 @@
         "window",
         cost_estimate=moved(4 * rows * width),
     )
-    return keys, turned, [up[1], down[1]]
+    return keys, turned, [up[1], down[1]], early
 
 
 def attend_kernel(
@@ -461,10 +463,11 @@
 
         pair = received[:, :, : 2 * HD]
         pair, received = lax.optimization_barrier((pair, received))
-        keys, turned, hops = pick_window(
-            pair, window_blocks, block_place, plane, window_places, window_counts
+        early = across(sent(received, 2 * HD, 0), "far", far)
+        keys, turned, hops, early = pick_window(
+            pair, window_blocks, block_place, plane, window_places, window_counts, early
         )
-        arrived = [across(sent(received, 2 * HD, 0), "far", far)]
+        arrived = [early]
         hops, later = lax.optimization_barrier((hops, later))
         received = in_plane(later)
         offset = 0

time: 183 us -> 185 us (1.011)
    ppermute x12, starting transfers between devices: 11.8 us -> 14.4 us  [across(): lax.ppermute(parts[at], axis, [(d, d ^ at) for d in range(size)])]
    ppermute x12, waiting for transfers between devices: 40.3 us -> 42.6 us  [across(): lax.ppermute(parts[at], axis, [(d, d ^ at) for d in range(size)])]
where the time goes in v1:
time: 185 us; the launch traced here: 182 us
  waiting for transfers between devices  77.9 us (42%)
  Pallas kernels  54 us (29%)
  starting transfers between devices  41.5 us (22%)
  local copies, waits for them, and re-layouts  4.65 us (3%)
  other arithmetic  2.72 us (1%)
    pallas_call x7, Pallas kernels, call(): pl.pallas_call(kernel, out_shape=outs, grid_spec=pltpu.PrefetchScalarGrid...  54 us
    ppermute x12, waiting for transfers between devices, across(): lax.ppermute(parts[at], axis, [(d, d ^ at) for d in range(size)])  42.6 us
    all_to_all x2, waiting for transfers between devices, in_plane(): lax.all_to_all(x, ('near', 'head'), split_axis=0, concat_axis=0, tiled=True)  14.6 us
    ppermute x12, starting transfers between devices, across(): lax.ppermute(parts[at], axis, [(d, d ^ at) for d in range(size)])  14.4 us
    ppermute x3, waiting for transfers between devices, pick_window(): up.append(lax.ppermute(up[-1], 'far', [(p, p + 1) for p in range(far - 1)]))  13.3 us
    ppermute x3, starting transfers between devices, pick_window(): lax.ppermute(down[-1], 'far', [(p + 1, p) for p in range(far - 1)])  9.48 us
    ppermute x3, starting transfers between devices, pick_window(): up.append(lax.ppermute(up[-1], 'far', [(p, p + 1) for p in range(far - 1)]))  8.88 us
    all_to_all x2, starting transfers between devices, in_plane(): lax.all_to_all(x, ('near', 'head'), split_axis=0, concat_axis=0, tiled=True)  8.75 us
  transfers between devices with their start and end apart: 20, of which 10 were waited for; matrix products, arithmetic and copies ran while one was open for 2% of the time, Pallas kernels for 27%

profile of v1, /device:TPU:14, one launch (start us, length us, event | category | flops | bytes accessed | tf_op | source)
XLA Modules:
  0.0 182.3 jit_solution(4843295794211647725)
XLA Ops:
  0.0 3.4 %split.1 = (bf16[8,128,768]{2,1,0:T(8,128)(2,1)}, bf16[8,128,512]{2,1,0:T(8,128)(2,1)}) custom-call(bf16[128,8192]{1,0:T(8,128)(2,1)} %query.1, bf16[128,1024]{1,0:T(8,128)(2,1)} %key.1, bf16[128,1024]{1,0:T(8,128)(2,1)} %value.1), custom_call_target="tpu_custom_call" | custom-call | bytes 5242880 | tf_op jit(solution)/shard_map/split/pallas_call | solution.py:26
  3.5 4.3 %all-to-all-start.3 = ((bf16[8,128,768]{2,1,0:T(8,128)(2,1)}), bf16[8,128,768]{2,1,0:T(8,128)(2,1)S(1)}, u32[]{:S(2)}, u32[]{:S(2)}) async-start(bf16[8,128,768]{2,1,0:T(8,128)(2,1)} %get-tuple-element.199), calls=%async_computation.3 | async-start | bytes 3145728 | tf_op jit(solution)/shard_map/all_to_all | solution.py:403
  11.9 14.6 %all-to-all-done.3 = bf16[8,128,768]{2,1,0:T(8,128)(2,1)S(1)} async-done(((bf16[8,128,768]{2,1,0:T(8,128)(2,1)}), bf16[8,128,768]{2,1,0:T(8,128)(2,1)S(1)}, u32[]{:S(2)}, u32[]{:S(2)}) %all-to-all-start.3) | async-done | bytes 1572896 | tf_op jit(solution)/shard_map/all_to_all | solution.py:403
  26.5 154.4 %conditional.1 = (bf16[256,4096]{1,0:T(8,128)(2,1)S(1)}) conditional(s32[]{:T(128)} %clamp.4, (s32[]{:T(128)}, bf16[64,16,768]{2,1,0:T(8,128)(2,1)S(1)}, s32[128]{0:T(128)S(1)}, s32[4]{0:T(128)S(1)}, s32[448]{0:T(512)S(1)}, /*index=5*/s32[8]{0:T(128)S(1)}, s32[128]{0:T(128)S(1)}, s32[4]{0:T(128)S(1)}, s32[4]{0:T(128)S(1)}, ...), branch_computations={%region_7.8_spmd, %region_8.9_spmd, %region_9.10_spmd} | conditional | flops 12884901888 | bytes 76547184 | solution.py:485
  26.6 3.5 %collective-permute-start.21 = (bf16[64,16,256]{2,1,0:T(8,128)(2,1)S(1)}, bf16[64,16,256]{2,1,0:T(8,128)(2,1)S(1)}, u32[]{:S(2)}, u32[]{:S(2)}) collective-permute-start(bf16[64,16,256]{2,1,0:T(8,128)(2,1)S(1)} %slice.7.refs_0_), channel_id=1, source_target_pairs={{0,8},{8,16},{16,24},{1,9},{9,17},{17,25},{2,10},{10,18},{18,26},{... | collective-permute-start | bytes 1572872 | tf_op jit(solution)/shard_map/cond/branch_1_fun/ppermute | solution.py:190
  30.1 2.4 %collective-permute-start.23 = (bf16[64,16,256]{2,1,0:T(8,128)(2,1)S(1)}, bf16[64,16,256]{2,1,0:T(8,128)(2,1)S(1)}, u32[]{:S(2)}, u32[]{:S(2)}) collective-permute-start(bf16[64,16,256]{2,1,0:T(8,128)(2,1)S(1)} %slice.7.refs_0_), channel_id=1, source_target_pairs={{8,0},{16,8},{24,16},{9,1},{17,9},{25,17},{10,2},{18,10},{26,18},{... | collective-permute-start | bytes 1572872 | tf_op jit(solution)/shard_map/cond/branch_1_fun/ppermute | solution.py:191
  32.5 9.6 %collective-permute-done.21.refs_1_ = bf16[64,16,256]{2,1,0:T(8,128)(2,1)S(1)} collective-permute-done((bf16[64,16,256]{2,1,0:T(8,128)(2,1)S(1)}, bf16[64,16,256]{2,1,0:T(8,128)(2,1)S(1)}, u32[]{:S(2)}, u32[]{:S(2)}) %collective-permute-start.21) | collective-permute-done | bytes 524320 | tf_op jit(solution)/shard_map/cond/branch_1_fun/ppermute | solution.py:190
  42.1 3.5 %collective-permute-start.22 = (bf16[64,16,256]{2,1,0:T(8,128)(2,1)S(1)}, bf16[64,16,256]{2,1,0:T(8,128)(2,1)}, u32[]{:S(2)}, u32[]{:S(2)}) collective-permute-start(bf16[64,16,256]{2,1,0:T(8,128)(2,1)S(1)} %collective-permute-done.21.refs_1_), channel_id=1, source_target_pairs={{0,8},{8,16},{16,24},{1,9},{9,17},{17,25},{2,10},{10,18},{18,26},{... | collective-permute-start | bytes 1572872 | tf_op jit(solution)/shard_map/cond/branch_1_fun/ppermute | solution.py:190
  45.6 3.1 %collective-permute-start.24 = (bf16[64,16,256]{2,1,0:T(8,128)(2,1)S(1)}, bf16[64,16,256]{2,1,0:T(8,128)(2,1)}, u32[]{:S(2)}, u32[]{:S(2)}) collective-permute-start(bf16[64,16,256]{2,1,0:T(8,128)(2,1)S(1)} %collective-permute-done.23.refs_4_), channel_id=1, source_target_pairs={{8,0},{16,8},{24,16},{9,1},{17,9},{25,17},{10,2},{18,10},{26,18},{... | collective-permute-start | bytes 1572872 | tf_op jit(solution)/shard_map/cond/branch_1_fun/ppermute | solution.py:191
  50.5 2.7 %collective-permute-start.19 = (bf16[24,16,512]{2,1,0:T(8,128)(2,1)}, bf16[24,16,512]{2,1,0:T(8,128)(2,1)}, u32[]{:S(2)}, u32[]{:S(2)}) collective-permute-start(bf16[24,16,512]{2,1,0:T(8,128)(2,1)} %get-tuple-element.124), channel_id=1, source_target_pairs={{0,16},{8,24},{16,0},{24,8},{1,17},{9,25},{17,1},{25,9},{2,18},{10... | collective-permute-start | bytes 1179656 | tf_op jit(solution)/shard_map/cond/branch_1_fun/ppermute | solution.py:396
  53.1 4.4 %all-to-all-start.1 = ((bf16[8,128,512]{2,1,0:T(8,128)(2,1)}), bf16[8,128,512]{2,1,0:T(8,128)(2,1)S(1)}, u32[]{:S(2)}, u32[]{:S(2)}) async-start(bf16[8,128,512]{2,1,0:T(8,128)(2,1)} %get-tuple-element.142), calls=%async_computation.1 | async-start | bytes 2097152 | tf_op jit(solution)/shard_map/cond/branch_1_fun/all_to_all | solution.py:403
  58.3 16.8 %collective-permute-done.18.refs_1_ = bf16[24,16,512]{2,1,0:T(8,128)(2,1)S(1)} collective-permute-done((bf16[24,16,512]{2,1,0:T(8,128)(2,1)}, bf16[24,16,512]{2,1,0:T(8,128)(2,1)S(1)}, u32[]{:S(2)}, u32[]{:S(2)}) %collective-permute-start.18) | collective-permute-done | bytes 393248 | tf_op jit(solution)/shard_map/cond/branch_1_fun/ppermute | solution.py:396
  75.2 8.2 %collective-permute-done.19.refs_2_ = bf16[24,16,512]{2,1,0:T(8,128)(2,1)} collective-permute-done((bf16[24,16,512]{2,1,0:T(8,128)(2,1)}, bf16[24,16,512]{2,1,0:T(8,128)(2,1)}, u32[]{:S(2)}, u32[]{:S(2)}) %collective-permute-start.19) | collective-permute-done | bytes 393248 | tf_op jit(solution)/shard_map/cond/branch_1_fun/ppermute | solution.py:396
  83.3 10.3 %collective-permute-done.20.refs_3_ = bf16[24,16,512]{2,1,0:T(8,128)(2,1)S(1)} collective-permute-done((bf16[24,16,512]{2,1,0:T(8,128)(2,1)}, bf16[24,16,512]{2,1,0:T(8,128)(2,1)S(1)}, u32[]{:S(2)}, u32[]{:S(2)}) %collective-permute-start.20) | collective-permute-done | bytes 393248 | tf_op jit(solution)/shard_map/cond/branch_1_fun/ppermute | solution.py:396
  95.6 4.0 %collective-permute-start.26 = (bf16[64,16,256]{2,1,0:T(8,128)(2,1)}, bf16[64,16,256]{2,1,0:T(8,128)(2,1)}, u32[]{:S(2)}, u32[]{:S(2)}) collective-permute-start(bf16[64,16,256]{2,1,0:T(8,128)(2,1)} %collective-permute-done.24.refs_5_), channel_id=1, source_target_pairs={{8,0},{16,8},{24,16},{9,1},{17,9},{25,17},{10,2},{18,10},{26,18},{... | collective-permute-start | bytes 1572872 | tf_op jit(solution)/shard_map/cond/branch_1_fun/ppermute | solution.py:191
  100.6 2.8 %pack.9 = (bf16[24,16,512]{2,1,0:T(8,128)(2,1)}, bf16[24,16,512]{2,1,0:T(8,128)(2,1)}, bf16[24,16,512]{2,1,0:T(8,128)(2,1)}, bf16[24,16,512]{2,1,0:T(8,128)(2,1)}) custom-call(s32[128]{0:T(128)S(1)} %get-tuple-element.118.source_ref, s32[4]{0:T(128)S(1)} %get-tuple-element.119.counts_ref, bf16[64,16,512]{2,1,0:T(8,128)(2,1)} %bitcast.14), custom_call_target="tpu_custom_call" | custom-call | bytes 2097152 | tf_op jit(solution)/shard_map/cond/branch_1_fun/pack/pallas_call | solution.py:26
  107.0 3.7 %collective-permute-done.25.refs_3_ = bf16[64,16,256]{2,1,0:T(8,128)(2,1)S(1)} collective-permute-done((bf16[64,16,256]{2,1,0:T(8,128)(2,1)}, bf16[64,16,256]{2,1,0:T(8,128)(2,1)S(1)}, u32[]{:S(2)}, u32[]{:S(2)}) %collective-permute-start.25) | collective-permute-done | bytes 524320 | tf_op jit(solution)/shard_map/cond/branch_1_fun/ppermute | solution.py:190
  110.7 7.4 %collective-permute-done.26.refs_6_ = bf16[64,16,256]{2,1,0:T(8,128)(2,1)} collective-permute-done((bf16[64,16,256]{2,1,0:T(8,128)(2,1)}, bf16[64,16,256]{2,1,0:T(8,128)(2,1)}, u32[]{:S(2)}, u32[]{:S(2)}) %collective-permute-start.26) | collective-permute-done | bytes 524320 | tf_op jit(solution)/shard_map/cond/branch_1_fun/ppermute | solution.py:191
  118.1 4.5 %window.4 = (bf16[3072,128]{1,0:T(8,128)(2,1)}, bf16[144,3072]{1,0:T(8,128)(2,1)}) custom-call(s32[448]{0:T(512)S(1)} %get-tuple-element.131.rows_ref, s32[8]{0:T(128)S(1)} %get-tuple-element.132.counts_ref, bf16[64,16,256]{2,1,0:T(8,128)(2,1)} %copy-done.4, bf16[64,16,256]{2,1,0:T(8,128)(2,1)} %copy-done.7, ...), custom_call_target="tpu_custom_call" | custom-call | bytes 3145728 | tf_op jit(solution)/shard_map/cond/branch_1_fun/window/pallas_call | solution.py:26
  122.6 20.0 %attend.8 = (bf16[256,512]{1,0:T(8,128)(2,1)}, bf16[256,512]{1,0:T(8,128)(2,1)}, bf16[256,512]{1,0:T(8,128)(2,1)}, bf16[256,512]{1,0:T(8,128)(2,1)}) custom-call(s32[128]{0:T(128)S(1)} %get-tuple-element.114.place_ref, s32[4]{0:T(128)S(1)} %get-tuple-element.115.counts_ref, s32[4]{0:T(128)S(1)} %get-tuple-element.116.lengths_ref, ...), custom_call_target="tpu_custom_call" | custom-call | flops 6442450944 | bytes 2097152 | tf_op jit(solution)/shard_map/cond/branch_1_fun/attend/pallas_call | solution.py:26
  142.6 2.3 %collective-permute-start.28 = (bf16[256,512]{1,0:T(8,128)(2,1)}, bf16[256,512]{1,0:T(8,128)(2,1)S(1)}, u32[]{:S(2)}, u32[]{:S(2)}) collective-permute-start(bf16[256,512]{1,0:T(8,128)(2,1)} %get-tuple-element.139), channel_id=1, source_target_pairs={{0,4},{2,6},{4,0},{6,2},{1,5},{3,7},{5,1},{7,3},{8,12},{10,14},{12... | collective-permute-start | bytes 786440 | tf_op jit(solution)/shard_map/cond/branch_1_fun/ppermute | solution.py:396
  147.3 20.1 %attend.9 = (bf16[256,512]{1,0:T(8,128)(2,1)}, bf16[256,512]{1,0:T(8,128)(2,1)}, bf16[256,512]{1,0:T(8,128)(2,1)}, bf16[256,512]{1,0:T(8,128)(2,1)}) custom-call(s32[128]{0:T(128)S(1)} %get-tuple-element.114.place_ref, s32[4]{0:T(128)S(1)} %get-tuple-element.115.counts_ref, s32[4]{0:T(128)S(1)} %get-tuple-element.116.lengths_ref, ...), custom_call_target="tpu_custom_call" | custom-call | flops 6442450944 | bytes 2097152 | tf_op jit(solution)/shard_map/cond/branch_1_fun/attend/pallas_call | solution.py:26
  170.9 3.1 %collective-permute-done.33.refs_5_ = bf16[256,512]{1,0:T(8,128)(2,1)S(1)} collective-permute-done((bf16[256,512]{1,0:T(8,128)(2,1)}, bf16[256,512]{1,0:T(8,128)(2,1)S(1)}, u32[]{:S(2)}, u32[]{:S(2)}) %collective-permute-start.33) | collective-permute-done | bytes 262176 | tf_op jit(solution)/shard_map/cond/branch_1_fun/ppermute | solution.py:396
  174.0 2.5 %collective-permute-done.34.refs_6_ = bf16[256,512]{1,0:T(8,128)(2,1)S(1)} collective-permute-done((bf16[256,512]{1,0:T(8,128)(2,1)}, bf16[256,512]{1,0:T(8,128)(2,1)S(1)}, u32[]{:S(2)}, u32[]{:S(2)}) %collective-permute-start.34) | collective-permute-done | bytes 262176 | tf_op jit(solution)/shard_map/cond/branch_1_fun/ppermute | solution.py:396
  (81 shorter events, 23.7 us)
Async XLA Ops:
  3.5 23.1 %copy-start.49 = (s32[4]{0:T(128)S(1)}, s32[4]{0:T(128)}, u32[]{:S(2)}) copy-start(s32[4]{0:T(128)} %param.12) | copy-start | bytes 52
  3.5 23.1 %all-to-all-start.3 = ((bf16[8,128,768]{2,1,0:T(8,128)(2,1)}), bf16[8,128,768]{2,1,0:T(8,128)(2,1)S(1)}, u32[]{:S(2)}, u32[]{:S(2)}) async-start(bf16[8,128,768]{2,1,0:T(8,128)(2,1)} %get-tuple-element.199), calls=%async_computation.3 | async-start | bytes 3145728 | tf_op jit(solution)/shard_map/all_to_all | solution.py:403
  26.6 76.8 %copy-start.4 = (bf16[64,16,256]{2,1,0:T(8,128)(2,1)}, bf16[64,16,256]{2,1,0:T(8,128)(2,1)S(1)}, u32[]{:S(2)}) copy-start(bf16[64,16,256]{2,1,0:T(8,128)(2,1)S(1)} %slice.7.refs_0_) | copy-start | bytes 1572868 | tf_op jit(solution)/shard_map/cond
  26.6 15.5 %collective-permute-start.21 = (bf16[64,16,256]{2,1,0:T(8,128)(2,1)S(1)}, bf16[64,16,256]{2,1,0:T(8,128)(2,1)S(1)}, u32[]{:S(2)}, u32[]{:S(2)}) collective-permute-start(bf16[64,16,256]{2,1,0:T(8,128)(2,1)S(1)} %slice.7.refs_0_), channel_id=1, source_target_pairs={{0,8},{8,16},{16,24},{1,9},{9,17},{17,25},{2,10},{10,18},{18,26},{... | collective-permute-start | bytes 1572872 | tf_op jit(solution)/shard_map/cond/branch_1_fun/ppermute | solution.py:190
  30.1 15.5 %collective-permute-start.23 = (bf16[64,16,256]{2,1,0:T(8,128)(2,1)S(1)}, bf16[64,16,256]{2,1,0:T(8,128)(2,1)S(1)}, u32[]{:S(2)}, u32[]{:S(2)}) collective-permute-start(bf16[64,16,256]{2,1,0:T(8,128)(2,1)S(1)} %slice.7.refs_0_), channel_id=1, source_target_pairs={{8,0},{16,8},{24,16},{9,1},{17,9},{25,17},{10,2},{18,10},{26,18},{... | collective-permute-start | bytes 1572872 | tf_op jit(solution)/shard_map/cond/branch_1_fun/ppermute | solution.py:191
  42.1 61.3 %copy-start.7 = (bf16[64,16,256]{2,1,0:T(8,128)(2,1)}, bf16[64,16,256]{2,1,0:T(8,128)(2,1)S(1)}, u32[]{:S(2)}) copy-start(bf16[64,16,256]{2,1,0:T(8,128)(2,1)S(1)} %collective-permute-done.21.refs_1_) | copy-start | bytes 1572868 | tf_op jit(solution)/shard_map/cond
  42.1 51.6 %collective-permute-start.22 = (bf16[64,16,256]{2,1,0:T(8,128)(2,1)S(1)}, bf16[64,16,256]{2,1,0:T(8,128)(2,1)}, u32[]{:S(2)}, u32[]{:S(2)}) collective-permute-start(bf16[64,16,256]{2,1,0:T(8,128)(2,1)S(1)} %collective-permute-done.21.refs_1_), channel_id=1, source_target_pairs={{0,8},{8,16},{16,24},{1,9},{9,17},{17,25},{2,10},{10,18},{18,26},{... | collective-permute-start | bytes 1572872 | tf_op jit(solution)/shard_map/cond/branch_1_fun/ppermute | solution.py:190
  45.6 57.8 %copy-start.9 = (bf16[64,16,256]{2,1,0:T(8,128)(2,1)}, bf16[64,16,256]{2,1,0:T(8,128)(2,1)S(1)}, u32[]{:S(2)}) copy-start(bf16[64,16,256]{2,1,0:T(8,128)(2,1)S(1)} %collective-permute-done.23.refs_4_) | copy-start | bytes 1572868 | tf_op jit(solution)/shard_map/cond
  45.6 48.1 %collective-permute-start.24 = (bf16[64,16,256]{2,1,0:T(8,128)(2,1)S(1)}, bf16[64,16,256]{2,1,0:T(8,128)(2,1)}, u32[]{:S(2)}, u32[]{:S(2)}) collective-permute-start(bf16[64,16,256]{2,1,0:T(8,128)(2,1)S(1)} %collective-permute-done.23.refs_4_), channel_id=1, source_target_pairs={{8,0},{16,8},{24,16},{9,1},{17,9},{25,17},{10,2},{18,10},{26,18},{... | collective-permute-start | bytes 1572872 | tf_op jit(solution)/shard_map/cond/branch_1_fun/ppermute | solution.py:191
  50.4 24.8 %collective-permute-start.18 = (bf16[24,16,512]{2,1,0:T(8,128)(2,1)}, bf16[24,16,512]{2,1,0:T(8,128)(2,1)S(1)}, u32[]{:S(2)}, u32[]{:S(2)}) collective-permute-start(bf16[24,16,512]{2,1,0:T(8,128)(2,1)} %get-tuple-element.123), channel_id=1, source_target_pairs={{0,8},{8,0},{16,24},{24,16},{1,9},{9,1},{17,25},{25,17},{2,10},{10... | collective-permute-start | bytes 1179656 | tf_op jit(solution)/shard_map/cond/branch_1_fun/ppermute | solution.py:396
  50.5 32.9 %collective-permute-start.19 = (bf16[24,16,512]{2,1,0:T(8,128)(2,1)}, bf16[24,16,512]{2,1,0:T(8,128)(2,1)}, u32[]{:S(2)}, u32[]{:S(2)}) collective-permute-start(bf16[24,16,512]{2,1,0:T(8,128)(2,1)} %get-tuple-element.124), channel_id=1, source_target_pairs={{0,16},{8,24},{16,0},{24,8},{1,17},{9,25},{17,1},{25,9},{2,18},{10... | collective-permute-start | bytes 1179656 | tf_op jit(solution)/shard_map/cond/branch_1_fun/ppermute | solution.py:396
  53.1 46.5 %all-to-all-start.1 = ((bf16[8,128,512]{2,1,0:T(8,128)(2,1)}), bf16[8,128,512]{2,1,0:T(8,128)(2,1)S(1)}, u32[]{:S(2)}, u32[]{:S(2)}) async-start(bf16[8,128,512]{2,1,0:T(8,128)(2,1)} %get-tuple-element.142), calls=%async_computation.1 | async-start | bytes 2097152 | tf_op jit(solution)/shard_map/cond/branch_1_fun/all_to_all | solution.py:403
  57.5 36.1 %collective-permute-start.20 = (bf16[24,16,512]{2,1,0:T(8,128)(2,1)}, bf16[24,16,512]{2,1,0:T(8,128)(2,1)S(1)}, u32[]{:S(2)}, u32[]{:S(2)}) collective-permute-start(bf16[24,16,512]{2,1,0:T(8,128)(2,1)} %get-tuple-element.125), channel_id=1, source_target_pairs={{0,24},{8,16},{16,8},{24,0},{1,25},{9,17},{17,9},{25,1},{2,26},{10... | collective-permute-start | bytes 1179656 | tf_op jit(solution)/shard_map/cond/branch_1_fun/ppermute | solution.py:396
  93.7 17.0 %collective-permute-start.25 = (bf16[64,16,256]{2,1,0:T(8,128)(2,1)}, bf16[64,16,256]{2,1,0:T(8,128)(2,1)S(1)}, u32[]{:S(2)}, u32[]{:S(2)}) collective-permute-start(bf16[64,16,256]{2,1,0:T(8,128)(2,1)} %collective-permute-done.22.refs_2_), channel_id=1, source_target_pairs={{0,8},{8,16},{16,24},{1,9},{9,17},{17,25},{2,10},{10,18},{18,26},{... | collective-permute-start | bytes 1572872 | tf_op jit(solution)/shard_map/cond/branch_1_fun/ppermute | solution.py:190
  95.6 22.5 %collective-permute-start.26 = (bf16[64,16,256]{2,1,0:T(8,128)(2,1)}, bf16[64,16,256]{2,1,0:T(8,128)(2,1)}, u32[]{:S(2)}, u32[]{:S(2)}) collective-permute-start(bf16[64,16,256]{2,1,0:T(8,128)(2,1)} %collective-permute-done.24.refs_5_), channel_id=1, source_target_pairs={{8,0},{16,8},{24,16},{9,1},{17,9},{25,17},{10,2},{18,10},{26,18},{... | collective-permute-start | bytes 1572872 | tf_op jit(solution)/shard_map/cond/branch_1_fun/ppermute | solution.py:191
  103.4 41.5 %collective-permute-start.30 = (bf16[24,16,512]{2,1,0:T(8,128)(2,1)}, bf16[24,16,512]{2,1,0:T(8,128)(2,1)S(1)}, u32[]{:S(2)}, u32[]{:S(2)}) collective-permute-start(bf16[24,16,512]{2,1,0:T(8,128)(2,1)} %get-tuple-element.144), channel_id=1, source_target_pairs={{0,8},{8,0},{16,24},{24,16},{1,9},{9,1},{17,25},{25,17},{2,10},{10... | collective-permute-start | bytes 1179656 | tf_op jit(solution)/shard_map/cond/branch_1_fun/ppermute | solution.py:396
  103.5 42.9 %collective-permute-start.31 = (bf16[24,16,512]{2,1,0:T(8,128)(2,1)}, bf16[24,16,512]{2,1,0:T(8,128)(2,1)S(1)}, u32[]{:S(2)}, u32[]{:S(2)}) collective-permute-start(bf16[24,16,512]{2,1,0:T(8,128)(2,1)} %get-tuple-element.145), channel_id=1, source_target_pairs={{0,16},{8,24},{16,0},{24,8},{1,17},{9,25},{17,1},{25,9},{2,18},{10... | collective-permute-start | bytes 1179656 | tf_op jit(solution)/shard_map/cond/branch_1_fun/ppermute | solution.py:396
  104.9 41.4 %collective-permute-start.32 = (bf16[24,16,512]{2,1,0:T(8,128)(2,1)}, bf16[24,16,512]{2,1,0:T(8,128)(2,1)S(1)}, u32[]{:S(2)}, u32[]{:S(2)}) collective-permute-start(bf16[24,16,512]{2,1,0:T(8,128)(2,1)} %get-tuple-element.146), channel_id=1, source_target_pairs={{0,24},{8,16},{16,8},{24,0},{1,25},{9,17},{17,9},{25,1},{2,26},{10... | collective-permute-start | bytes 1179656 | tf_op jit(solution)/shard_map/cond/branch_1_fun/ppermute | solution.py:396
  142.6 26.9 %collective-permute-start.27 = (bf16[256,512]{1,0:T(8,128)(2,1)}, bf16[256,512]{1,0:T(8,128)(2,1)S(1)}, u32[]{:S(2)}, u32[]{:S(2)}) collective-permute-start(bf16[256,512]{1,0:T(8,128)(2,1)} %get-tuple-element.138), channel_id=1, source_target_pairs={{0,2},{2,0},{4,6},{6,4},{1,3},{3,1},{5,7},{7,5},{8,10},{10,8},{12,... | collective-permute-start | bytes 786440 | tf_op jit(solution)/shard_map/cond/branch_1_fun/ppermute | solution.py:396
  142.6 28.3 %collective-permute-start.28 = (bf16[256,512]{1,0:T(8,128)(2,1)}, bf16[256,512]{1,0:T(8,128)(2,1)S(1)}, u32[]{:S(2)}, u32[]{:S(2)}) collective-permute-start(bf16[256,512]{1,0:T(8,128)(2,1)} %get-tuple-element.139), channel_id=1, source_target_pairs={{0,4},{2,6},{4,0},{6,2},{1,5},{3,7},{5,1},{7,3},{8,12},{10,14},{12... | collective-permute-start | bytes 786440 | tf_op jit(solution)/shard_map/cond/branch_1_fun/ppermute | solution.py:396
  144.9 26.0 %collective-permute-start.29 = (bf16[256,512]{1,0:T(8,128)(2,1)}, bf16[256,512]{1,0:T(8,128)(2,1)S(1)}, u32[]{:S(2)}, u32[]{:S(2)}) collective-permute-start(bf16[256,512]{1,0:T(8,128)(2,1)} %get-tuple-element.140), channel_id=1, source_target_pairs={{0,6},{2,4},{4,2},{6,0},{1,7},{3,5},{5,3},{7,1},{8,14},{10,12},{12... | collective-permute-start | bytes 786440 | tf_op jit(solution)/shard_map/cond/branch_1_fun/ppermute | solution.py:396
  167.4 6.6 %collective-permute-start.33 = (bf16[256,512]{1,0:T(8,128)(2,1)}, bf16[256,512]{1,0:T(8,128)(2,1)S(1)}, u32[]{:S(2)}, u32[]{:S(2)}) collective-permute-start(bf16[256,512]{1,0:T(8,128)(2,1)} %get-tuple-element.148), channel_id=1, source_target_pairs={{0,2},{2,0},{4,6},{6,4},{1,3},{3,1},{5,7},{7,5},{8,10},{10,8},{12,... | collective-permute-start | bytes 786440 | tf_op jit(solution)/shard_map/cond/branch_1_fun/ppermute | solution.py:396
  168.0 8.5 %collective-permute-start.34 = (bf16[256,512]{1,0:T(8,128)(2,1)}, bf16[256,512]{1,0:T(8,128)(2,1)S(1)}, u32[]{:S(2)}, u32[]{:S(2)}) collective-permute-start(bf16[256,512]{1,0:T(8,128)(2,1)} %get-tuple-element.149), channel_id=1, source_target_pairs={{0,4},{2,6},{4,0},{6,2},{1,5},{3,7},{5,1},{7,3},{8,12},{10,14},{12... | collective-permute-start | bytes 786440 | tf_op jit(solution)/shard_map/cond/branch_1_fun/ppermute | solution.py:396
  169.5 8.7 %collective-permute-start.35 = (bf16[256,512]{1,0:T(8,128)(2,1)}, bf16[256,512]{1,0:T(8,128)(2,1)S(1)}, u32[]{:S(2)}, u32[]{:S(2)}) collective-permute-start(bf16[256,512]{1,0:T(8,128)(2,1)} %get-tuple-element.150), channel_id=1, source_target_pairs={{0,6},{2,4},{4,2},{6,0},{1,7},{3,5},{5,3},{7,1},{8,14},{10,12},{12... | collective-permute-start | bytes 786440 | tf_op jit(solution)/shard_map/cond/branch_1_fun/ppermute | solution.py:396
  (16 other events, 72.9 us)
